TPU v7x, 32 devices: a whole 2x2x4 slice. The times are simulated.
32 devices in a mesh: ctx: 4 (over z), fsdp: 8 (over y, x, core).
Axes of the slice: x: 2, y: 2, z: 4, core: 2. Of those that a mesh axis runs over, the one named last changes fastest.
Arguments:
- hidden_in: bfloat16 [8, 1024, 1536], P('fsdp', 'ctx'), may hold values from -6 to 6
- w_qkv: bfloat16 [1536, 2048], P('fsdp'), may hold values from -0.15625 to 0.15625
- b_qkv: bfloat16 [2048], P('fsdp'), may hold values from -3 to 3
- w_out: bfloat16 [1536, 1536], P('fsdp'), may hold values from -1 to 1
- w_gate_up: bfloat16 [1536, 17920], P('fsdp'), may hold values from -0.15625 to 0.15625
- w_down: bfloat16 [8960, 1536], P('fsdp'), may hold values from -0.0625 to 0.0625
- gain_attn: bfloat16 [1536], P('fsdp'), may hold values from 0.5 to 1.5
- gain_mlp: bfloat16 [1536], P('fsdp'), may hold values from 0.5 to 1.5
- block_order: int32 [8, 8], P('fsdp'), may hold values from 0 to 7, as said below
- cotangent: bfloat16 [8, 1024, 1536], P('fsdp', 'ctx'), may hold values from -6 to 6
Outputs:
- hidden_out: bfloat16 [8, 1024, 1536], P('fsdp', 'ctx')
- grad_hidden: bfloat16 [8, 1024, 1536], P('fsdp', 'ctx')
- grad_w_qkv: float32 [1536, 2048], P('fsdp')
- grad_b_qk: float32 [1792], P('fsdp')
- grad_b_v: float32 [256], P('fsdp')
- grad_w_out: float32 [1536, 1536], P('fsdp')
- grad_w_gate_up: float32 [1536, 17920], P('fsdp')
- grad_w_down: float32 [8960, 1536], P('fsdp')
- grad_gain_attn: float32 [1536], P('fsdp')
- grad_gain_mlp: float32 [1536], P('fsdp')
Inputs may be any that keep to these rules, and one draw needn't show every extreme that they name: `block_order`: each row holds every number below 8 once: the places of the stored blocks of a sequence of 128 tokens each.
All inputs are finite; a program needn't handle non-finite values.
Results may differ from a plain program's by a relative error of at most 0.025.
Values may be sent and summed in bfloat16 or wider, within the bound.
A program may use at most 448 MiB of HBM per device.

v0:
```python
import functools

import jax
import jax.numpy as jnp
from jax import lax
from jax.experimental import pallas as pl
from jax.experimental.pallas import tpu as pltpu
from jax.sharding import PartitionSpec as P

HEADS = 12
KV_HEADS = 2
HEAD_DIM = 128
EPSILON = 1e-06
THETA = 1000000.0
MASKED = -1e30
BF = jnp.bfloat16
F32 = jnp.float32


def dot(a, b):
    return jnp.dot(a, b, preferred_element_type=F32)


def dot_bt(a, b):
    return lax.dot_general(a, b, (((1,), (1,)), ((), ())), preferred_element_type=F32)


def dot_at(a, b):
    return lax.dot_general(a, b, (((0,), (0,)), ((), ())), preferred_element_type=F32)


def angle_tables(places):
    half_dim = HEAD_DIM // 2
    freqs = THETA ** (-(jnp.arange(half_dim).astype(F32) * 2.0 / HEAD_DIM))
    angles = places.astype(F32)[:, None] * freqs[None, :]
    return (jnp.cos(angles), jnp.sin(angles))


def half_rows(rows):
    return -(-rows // 32) * 16


def pieces_of(columns, width, rows, room):
    n = next(n for n in range(1, columns) if columns % (128 * n) == 0 and columns // n <= width)
    assert n * rows <= room
    return n


def pack(k, nz, nf, ff, unit, upad, rows, width, held, out):
    for h in range(2):
        for f in range(nf):
            src = h * ff + f * (ff // nf) + k * unit
            dst = (h * nf + f) * upad
            done = 0
            while done < unit:
                piece, at = divmod(src + done, width)
                n = min(unit - done, width - at)
                out[:, dst + done : dst + done + n] = held[
                    piece * rows : (piece + 1) * rows, at : at + n
                ]
                done += n
            if upad > unit:
                out[:, dst + unit : dst + upad] = jnp.zeros((rows, upad - unit), out.dtype)


def unpack_kernel(nz, nf, ff, unit, upad, *refs):
    out_ref = refs[-1]
    for k in range(nz):
        for h in range(2):
            for f in range(nf):
                src = f * upad
                dst = h * ff + f * (ff // nf) + k * unit
                part = refs[h * nz + k]
                out_ref[:, dst : dst + unit] = part[:, src : src + unit].astype(F32)


def unpack(gate, up, nz, nf, ff):
    rows, wide = gate.shape[0] // nz, gate.shape[1]
    step = 32
    specs = [
        pl.BlockSpec((step, wide), lambda i, k=k: (k * (rows // step) + i, 0)) for k in range(nz)
    ]
    return pl.pallas_call(
        functools.partial(unpack_kernel, nz, nf, ff, ff // (nf * nz), wide // nf),
        grid=(rows // step,),
        in_specs=specs * 2,
        out_specs=pl.BlockSpec((step, 2 * ff), lambda i: (i, 0)),
        out_shape=jax.ShapeDtypeStruct((rows, 2 * ff), F32),
    )(*[gate] * nz, *[up] * nz)


def finish_kernel(nz, nf, ff, unit, upad, cuts, *refs):
    gates, ups = refs[:nz], refs[nz : 2 * nz]
    down, attn, tiny, hid, gh = refs[2 * nz : 2 * nz + 5]
    gu_out, down_out, qkv_out, out_out, hid_out, gh_out, *tiny_outs = refs[2 * nz + 5 :]
    unpack_kernel(nz, nf, ff, unit, upad, *gates, *ups, gu_out)
    down_out[...] = down[0:unit, :].astype(F32)
    d = out_out.shape[1]
    qkv_out[...] = attn[:, d:].astype(F32)
    out_out[...] = attn[:, :d].astype(F32)
    hid_out[...] = hid[...]
    gh_out[...] = gh[...]

    @pl.when(pl.program_id(0) == 0)
    def _():
        for out, lo, hi in zip(tiny_outs, cuts, cuts[1:]):
            out[...] = tiny[0:1, lo:hi]


def finish(gate, up, down, attn, tiny, hid, gh, nz, nf, ff, cuts):
    rows, wide = gate.shape[0] // nz, gate.shape[1]
    unit, upad, d = ff // (nf * nz), wide // nf, hid.shape[1]
    step = rows // nz
    along = [
        pl.BlockSpec((step, wide), lambda i, k=k: (k * (rows // step) + i, 0)) for k in range(nz)
    ]
    part = hid.shape[0] // nz

    def by_step(r, c):
        return pl.BlockSpec((r, c), lambda i: (i, 0))

    def still(c):
        return pl.BlockSpec((1, c), lambda i: (0, 0))

    qkv = attn.shape[1] - d
    sizes = [hi - lo for lo, hi in zip(cuts, cuts[1:])]
    out = jax.ShapeDtypeStruct
    return pl.pallas_call(
        functools.partial(finish_kernel, nz, nf, ff, unit, upad, cuts),
        grid=(nz,),
        in_specs=along * 2
        + [
            by_step(upad, d),
            by_step(step, d + qkv),
            pl.BlockSpec(tiny.shape, lambda i: (0, 0)),
            by_step(part, d),
            by_step(part, d),
        ],
        out_specs=[
            by_step(step, 2 * ff),
            by_step(unit, d),
            by_step(step, qkv),
            by_step(step, d),
            by_step(part, d),
            by_step(part, d),
        ]
        + [still(n) for n in sizes],
        out_shape=[
            out((rows, 2 * ff), F32),
            out((nz * unit, d), F32),
            out((rows, qkv), F32),
            out((rows, d), F32),
            out(hid.shape, BF),
            out(hid.shape, BF),
        ]
        + [out((1, n), F32) for n in sizes],
        compiler_params=pltpu.CompilerParams(vmem_limit_bytes=VMEM_LIMIT),
    )(*[gate] * nz, *[up] * nz, down, attn, tiny, hid, gh)


MESH = pl.DeviceIdType.MESH
VMEM_LIMIT = 63 * 2**20


def remote(src, dst, send, recv, z, f):
    return pltpu.make_async_remote_copy(
        src_ref=src, dst_ref=dst, send_sem=send, recv_sem=recv, device_id=(z, f), device_id_type=MESH
    )


def rows_at(ref, index, count):
    return ref.at[pl.ds(pl.multiple_of(index * count, count), count)]


class PlaneGather:
    def __init__(self, src, dst, rows, nf, z, me, send, recv, local, base, bounce=None):
        self.src, self.dst, self.rows, self.nf, self.z, self.me = src, dst, rows, nf, z, me
        self.send, self.recv, self.base = send, recv, base
        home = rows_at(dst, me, rows)
        if bounce is None:
            self.local = (pltpu.make_async_copy(src, home, local),)
        else:
            self.local = (
                pltpu.make_async_copy(src, bounce, local),
                pltpu.make_async_copy(bounce, home, local),
            )
        self.sent = []
        self.cut = half_rows(rows)
        self.swaps = {}

    @staticmethod
    def sems(nf):
        return 2 * nf

    def slot(self, k, lo=0, hi=None):
        hi = self.rows if hi is None else hi
        start = pl.multiple_of((self.me ^ k) * self.rows, 16) + lo
        return self.dst.at[pl.ds(pl.multiple_of(start, 16), hi - lo)]

    def push(self, index, src, dst, flip_by):
        copy = remote(
            src, dst, self.send.at[self.base + index], self.recv.at[self.base + index],
            self.z, self.me ^ flip_by,
        )
        copy.start()
        self.sent.append(copy)
        return copy

    def begin(self):
        self.local[0].start()
        self.direct = {}
        for k in (2, 4) if self.nf == 8 else range(2, self.nf, 2):
            self.direct[k] = self.push(k, self.src, self.slot(0), k)
        self.swaps[0] = self.push(1, self.src, self.slot(0), 1)

    def swap(self, k):
        self.swaps[k] = self.push(k + 1, self.slot(k), self.slot(k), 1)

    def middle(self):
        for one, two in zip(self.local, self.local[1:]):
            one.wait()
            two.start()
        for k, copy in self.direct.items():
            copy.wait_recv()
            if self.nf == 8:
                if k == 2:
                    self.far_a = self.push(6, self.slot(2, 0, self.cut), self.slot(2, 0, self.cut), 4)
                elif self.cut < self.rows:
                    self.far_b = self.push(
                        8, self.slot(4, self.cut), self.slot(4, self.cut), 2
                    )
            self.swap(k)

    def late(self):
        if self.nf == 8:
            self.far_a.wait_recv()
            if self.cut < self.rows:
                self.far_b.wait_recv()
            self.swap(6)

    def finish(self):
        self.local[-1].wait()
        for copy in self.swaps.values():
            copy.wait_recv()

    def drain(self):
        for copy in self.sent:
            copy.wait_send()


class Chain:
    def __init__(self, buf, rows, nz, z, me, send, recv, base):
        self.buf, self.rows, self.nz, self.z, self.me = buf, rows, nz, z, me
        self.send, self.recv, self.base = send, recv, base

    @staticmethod
    def sems(nz):
        return nz + 2

    def copy(self, j, sem, step, src=None):
        slot = rows_at(self.buf, j, self.rows)
        return remote(
            slot if src is None else src, slot, self.send.at[self.base + sem], self.recv.at[self.base + j], self.z + step, self.me
        )

    def order(self, k):
        z, nz = self.z, self.nz
        below, above = z, nz - 1 - z
        m = jnp.minimum(below, above)
        near = jnp.where(k % 2 == 1, z - (k + 1) // 2, z + k // 2)
        far = jnp.where(above > below, z + (k - m), z - (k - m))
        return jnp.where(k <= 2 * m, near, far)

    def begin(self, src=None):
        z, nz = self.z, self.nz

        @pl.when(z < nz - 1)
        def _():
            self.copy(z, nz, 1, src).start()

        @pl.when(z > 0)
        def _():
            self.copy(z, nz + 1, -1, src).start()

    def passing(self, j):
        z, nz = self.z, self.nz
        return jnp.logical_and(j < z, z < nz - 1), jnp.logical_and(j > z, z > 0)

    def forward(self, k):
        j = self.order(k)
        up, down = self.passing(j)

        @pl.when(up)
        def _():
            self.copy(j, j, 1).wait_recv()
            self.copy(j, j, 1).start()

        @pl.when(down)
        def _():
            self.copy(j, j, -1).wait_recv()
            self.copy(j, j, -1).start()

    def arrive(self, k):
        j = self.order(k)
        up, down = self.passing(j)

        @pl.when(jnp.logical_not(jnp.logical_or(up, down)))
        def _():
            self.copy(j, j, 0).wait_recv()

    def drain(self):
        z, nz = self.z, self.nz

        @pl.when(z < nz - 1)
        def _():
            self.copy(z, nz, 1).wait_send()

        @pl.when(z > 0)
        def _():
            self.copy(z, nz + 1, -1).wait_send()

        def one(k, carry):
            j = self.order(k)
            up, down = self.passing(j)

            @pl.when(jnp.logical_or(up, down))
            def _():
                self.copy(j, j, 0).wait_send()

            return carry

        lax.fori_loop(1, nz, one, 0)


class Scatter:
    def __init__(self, src, c0, rows, cols, recv4, land, inside, nf, z, me, send, recv, base, own=None, sems=None):
        self.src, self.c0, self.rows, self.cols = src, c0, rows, cols
        self.recv4, self.land, self.inside = recv4, land, inside
        self.nf, self.z, self.me, self.send, self.recv, self.base = nf, z, me, send, recv, base
        self.chips, self.chip, self.core = nf // 2, me // 2, me % 2
        self.cut = half_rows(rows)
        self.sent = []
        self.got = {}
        self.own, self.own_sems = own, sems

    @staticmethod
    def sems(nf):
        return nf

    def push(self, index, src, dst, flip_by):
        copy = remote(
            src, dst, self.send.at[self.base + index], self.recv.at[self.base + index],
            self.z, self.me ^ flip_by,
        )
        copy.start()
        self.sent.append(copy)
        self.got[index] = copy

    def mine(self, ref, start, n):
        return ref.at[pl.ds(pl.multiple_of(start, 16), n)]

    def block(self, k, lo=0, hi=None):
        hi = self.rows if hi is None else hi
        return self.mine(self.recv4, (self.chip ^ k) * self.rows + lo, hi - lo)

    def swap(self):
        for p in range(self.chips):
            start = pl.multiple_of((2 * p + 1 - self.core) * self.rows, 16)
            src = self.src.at[pl.ds(start, self.rows), pl.ds(self.c0, self.cols)]
            self.push(p, src, self.mine(self.recv4, p * self.rows, self.rows), 1)

    def merge(self):
        rows, cols = self.rows, self.cols
        if self.own is not None:
            for p in range(min(2, self.chips)):
                self.fetch(p).start()
        for p in range(self.chips):
            self.got[p].wait_recv()
        if self.inside:
            for p in range(self.chips):
                start = pl.multiple_of((2 * p + self.core) * rows, 16)
                if self.own is None:
                    own, first = self.src, start
                else:
                    self.fetch(p).wait()
                    own, first = self.own, p % 2 * rows
                step = rows if rows <= 96 else rows // 2
                for i in range(0, rows, step):
                    where = pl.ds(p * rows + i, step)
                    part = own[pl.ds(pl.multiple_of(first + i, 16), step), pl.ds(0, cols)]
                    self.recv4[where, :] = (
                        self.recv4[where, :].astype(F32) + part.astype(F32)
                    ).astype(BF)
                if self.own is not None and p + 2 < self.chips:
                    self.fetch(p + 2).start()
            return
        step = rows if rows <= 96 else rows // 2
        n = rows // step
        core, col = self.core, self.c0 // cols
        own = pl.BlockSpec((step, cols), lambda p, i: ((2 * p + core) * n + i, col))
        held = pl.BlockSpec((step, cols), lambda p, i: (p * n + i, 0))
        pltpu.emit_pipeline(
            add_two, grid=(self.chips, n), in_specs=[own, held], out_specs=[held]
        )(self.src, self.recv4, self.recv4)

    def fetch(self, p):
        start = pl.multiple_of((2 * p + self.core) * self.rows, 16)
        return pltpu.make_async_copy(
            self.src.at[pl.ds(start, self.rows), pl.ds(self.c0, self.cols)],
            self.own.at[pl.ds(p % 2 * self.rows, self.rows)],
            self.own_sems.at[p % 2],
        )

    def add(self, out, parts, n):
        if self.inside:
            total = parts[0][...].astype(F32)
            for part in parts[1:]:
                total = total + part[...].astype(F32)
            out[...] = total.astype(BF)
            return
        step = n if n <= 96 else n // 2
        spec = pl.BlockSpec((step, self.cols), lambda i: (i, 0))
        body = add_two if len(parts) == 2 else add_all
        pltpu.emit_pipeline(
            body, grid=(n // step,), in_specs=[spec] * len(parts), out_specs=[spec]
        )(*parts, out)

    def first(self):
        base, rows, cut = self.chips, self.rows, self.cut
        if self.nf == 8:
            self.push(base, self.block(3, 0, cut), self.land.at[pl.ds(0, cut)], 2)
            self.push(base + 1, self.block(3, cut), self.land.at[pl.ds(cut, rows - cut)], 4)
        else:
            for k in range(1, self.chips):
                self.push(base + k - 1, self.block(k), self.land.at[pl.ds((k - 1) * rows, rows)], 2 * k)

    def second(self):
        if self.nf != 8:
            return
        base, rows, cut = self.chips, self.rows, self.cut
        self.got[base].wait_recv()
        to_y = self.block(2, 0, cut)
        self.add(to_y, [to_y, self.land.at[pl.ds(0, cut)]], cut)
        self.push(base + 3, self.block(2), self.land.at[pl.ds(2 * rows, rows)], 4)
        self.got[base + 1].wait_recv()
        to_x = self.block(1, cut)
        self.add(to_x, [to_x, self.land.at[pl.ds(cut, rows - cut)]], rows - cut)
        self.push(base + 2, self.block(1), self.land.at[pl.ds(rows, rows)], 2)

    def last(self, out):
        base, rows = self.chips, self.rows
        if self.nf == 8:
            incoming = [(base + 2, rows), (base + 3, 2 * rows)]
        else:
            incoming = [(base + k - 1, (k - 1) * rows) for k in range(1, self.chips)]
        for index, _ in incoming:
            self.got[index].wait_recv()
        parts = [self.block(0)] + [self.land.at[pl.ds(at, rows)] for _, at in incoming]
        self.add(out, parts, rows)

    def drain(self):
        for copy in self.sent:
            copy.wait_send()
        self.sent = []


def add_two(a, b, out):
    out[...] = (a[...].astype(F32) + b[...].astype(F32)).astype(BF)


def add_all(*refs):
    total = refs[0][...].astype(F32)
    for ref in refs[1:-1]:
        total = total + ref[...].astype(F32)
    refs[-1][...] = total.astype(BF)


def greet_ctx_and_plane(nz, nf, z, me):
    barrier = pltpu.get_barrier_semaphore()
    flips = (1, 2, 4) if nf == 8 else (1,) + tuple(range(2, nf, 2))
    for k in flips:
        pl.semaphore_signal(barrier, inc=1, device_id=(z, me ^ k), device_id_type=MESH)

    @pl.when(z < nz - 1)
    def _():
        pl.semaphore_signal(barrier, inc=1, device_id=(z + 1, me), device_id_type=MESH)

    @pl.when(z > 0)
    def _():
        pl.semaphore_signal(barrier, inc=1, device_id=(z - 1, me), device_id_type=MESH)

    inner = jnp.logical_and(z > 0, z < nz - 1)

    @pl.when(inner)
    def _():
        pl.semaphore_wait(barrier, len(flips) + 2)

    @pl.when(jnp.logical_not(inner))
    def _():
        pl.semaphore_wait(barrier, len(flips) + 1)


def loop(n, body):
    def step(i, carry):
        body(i)
        return carry

    lax.fori_loop(0, n, step, 0)


def at128(i, n):
    return i * n if isinstance(i, int) else pl.multiple_of(i * n, n)


def turn(t, cos2, sin2):
    return t * cos2 + pltpu.roll(t, HEAD_DIM // 2, 1) * sin2


def front_kernel(
    dims,
    wq, sm, wo, w_gu, w_dn, x_ref, g_ref, cos_ref, sin_ref, qpos_ref, kpos_ref,
    wq_all, wo_all, q_ref, kv_out, o_ref, lse_ref, mid_ref, dx_ref, gain_ref, dwgu, dpart, d_own, dwd, r0, l0,
    stage, gu, dnb, g_all, x_all, act, dgu, smb, kv, bias, ybuf, packed, down, send, recv, local,
):
    nz, nf, rows, d, ff, wide, upad, nb, ng = dims
    z, me = lax.axis_index("ctx"), lax.axis_index("fsdp")
    q_width, k_width = HEADS * HEAD_DIM, KV_HEADS * HEAD_DIM
    qkv = q_width + 2 * k_width
    scale = HEAD_DIM ** (-0.5)
    wr = d // nf
    per = PlaneGather.sems(nf)
    q_cols, kv_cols = pl.ds(0, q_width), pl.ds(q_width, 2 * k_width)
    plane = [
        PlaneGather(src, dst, r, nf, z, me, send, recv, local.at[i], i * per, bounce)
        for i, (src, dst, r, bounce) in enumerate(
            [
                (wq.at[:, q_cols], wq_all.at[:, q_cols], wr, ybuf.at[pl.ds(wr, wr)]),
                (wq.at[:, kv_cols], wq_all.at[:, kv_cols], wr, ybuf.at[pl.ds(0, wr), pl.ds(0, 2 * k_width)]),
                (sm, smb, 16, None),
                (wo, wo_all, wr, ybuf.at[pl.ds(0, wr)]),
                (packed, gu, wr, None),
                (down, dnb, upad, None),
            ]
        )
    ]
    p_q, p_kv, p_s, p_o, p_gu, p_d = plane
    base = len(plane) * per
    chain = [
        Chain(buf, rows, nz, z, me, send, recv, base + i * Chain.sems(nz))
        for i, buf in enumerate([g_all, kv, x_all])
    ]
    c_g, c_kv, c_x = chain
    base += len(chain) * Chain.sems(nz)
    s_d = Scatter(dwd, 0, upad, d, r0, l0, False, nf, z, me, send, recv, base)
    base += Scatter.sems(nf)
    spare = len(plane)

    unit = ff // (nf * nz)
    n = pieces_of(2 * ff, 2 * wide, wr, nz * rows)
    width = 2 * ff // n
    loads = [
        pltpu.make_async_copy(
            w_gu.at[:, pl.ds(i * width, width)],
            dgu.at[pl.ds(i * wr, wr), pl.ds(0, width)],
            local.at[spare + 1 + i],
        )
        for i in range(n)
    ]
    fetched = upad + 16
    down_in = act.at[pl.ds(0, fetched), pl.ds(0, d)] if wide >= d else dgu.at[pl.ds(n * wr, fetched), pl.ds(0, d)]

    def down_load(k):
        start = min(unit * k // 16 * 16, ff // nf - fetched)
        copy = pltpu.make_async_copy(w_dn.at[pl.ds(start, fetched)], down_in, local.at[spare + 1 + n])
        return copy, unit * k - start

    def part_loads():
        for copy in loads:
            copy.start()
        for k in range(nz):

            @pl.when(z == k)
            def _():
                down_load(k)[0].start()

    def part_pack():
        for copy in loads:
            copy.wait()
        for k in range(nz):

            @pl.when(z == k)
            def _():
                pack(k, nz, nf, ff, unit, upad, wr, width, dgu, packed)
                copy, off = down_load(k)
                copy.wait()
                down[0:unit, :] = down_in[...].astype(F32)[off : off + unit].astype(BF)
                if upad > unit:
                    down[unit:upad, :] = jnp.zeros((upad - unit, d), BF)

    g_copy = pltpu.make_async_copy(g_ref, rows_at(g_all, z, rows), local.at[spare])
    g_copy.start()
    greet_ctx_and_plane(nz, nf, z, me)
    p_s.begin()
    p_kv.begin()
    g_copy.wait()
    c_g.begin()
    part_loads()

    x = x_ref[...].astype(F32)
    inverse = lax.rsqrt(jnp.mean(x * x, -1, keepdims=True) + EPSILON)

    p_s.middle()
    p_kv.middle()
    p_q.begin()
    p_s.late()
    p_kv.late()
    p_s.finish()
    for f in range(nf):
        row = smb[f * 16 : (f + 1) * 16, :].astype(F32)[0:1]
        bias[0:1, f * nb : (f + 1) * nb] = row[:, :nb]
        gain_ref[0:1, f * ng : (f + 1) * ng] = row[:, nb : nb + ng]
        gain_ref[1:2, f * ng : (f + 1) * ng] = row[:, nb + ng : nb + 2 * ng]
    normed = (x * inverse * gain_ref[0:1, :]).astype(BF)
    x_all[pl.ds(at128(z, rows), rows), :] = normed

    def fetch_qkv(c0, n):
        copy = pltpu.make_async_copy(
            wq_all.at[:, pl.ds(c0, n)], stage.at[pl.ds(0, d), pl.ds(c0, n)], local.at[spare]
        )
        copy.start()
        copy.wait()

    p_kv.finish()
    fetch_qkv(q_width, 2 * k_width)

    def project(t):
        c0 = at128(t, 2 * HEAD_DIM)
        y = dot(
            x_all[pl.ds(at128(z, rows), rows), :], stage[pl.ds(0, d), pl.ds(c0, 2 * HEAD_DIM)]
        ) + bias[0:1, pl.ds(c0, 2 * HEAD_DIM)]
        return y, c0

    def project_v(t):
        y, c0 = project(t)
        kv[pl.ds(at128(z, rows), rows), pl.ds(pl.multiple_of(c0 - q_width, 256), 256)] = y.astype(BF)

    def turned(y):
        halves = [
            turn(y[:, h * HEAD_DIM : (h + 1) * HEAD_DIM], cos_ref[...], sin_ref[...]).astype(BF)
            for h in range(2)
        ]
        return jnp.concatenate(halves, 1)

    project_v((q_width + k_width) // 256)
    y, _ = project(q_width // 256)
    kv[pl.ds(at128(z, rows), rows), 0:k_width] = turned(y)
    c_kv.begin()
    p_q.middle()
    p_o.begin()
    part_pack()
    for k in range(1, nz - 1):
        c_kv.forward(k)
    p_q.late()
    p_q.finish()
    fetch_qkv(0, q_width)
    c_kv.forward(nz - 1)

    def project_q(t):
        y, c0 = project(t)
        q_ref[:, pl.ds(c0, 256)] = turned(y)

    loop(q_width // 256, project_q)
    p_o.middle()
    p_gu.begin()
    for k in range(1, nz):
        c_kv.arrive(k)
    for k in range(1, nz - 1):
        c_g.forward(k)

    lanes = lax.broadcasted_iota(jnp.int32, (rows, HEAD_DIM), 1)
    lse_ref[...] = jnp.zeros_like(lse_ref)

    def head(h):
        c0 = at128(h, HEAD_DIM)
        kc = at128(h // (HEADS // KV_HEADS), HEAD_DIM)
        vc = pl.multiple_of(kc + k_width, HEAD_DIM)
        s = dot_bt(q_ref[:, pl.ds(c0, HEAD_DIM)], kv[:, pl.ds(kc, HEAD_DIM)]) * scale
        s = jnp.where(kpos_ref[...] <= qpos_ref[...], s, MASKED)
        top = jnp.max(s, -1, keepdims=True)
        p = jnp.exp(s - top)
        total = jnp.sum(p, -1, keepdims=True)
        o = dot(p.astype(BF), kv[:, pl.ds(vc, HEAD_DIM)]) / total
        o_ref[:, pl.ds(c0, HEAD_DIM)] = o.astype(BF)
        lse_ref[...] = jnp.where(lanes == h, top + jnp.log(total), lse_ref[...])

    loop(HEADS, head)
    p_o.late()
    p_o.finish()
    fetch = pltpu.make_async_copy(wo_all, stage.at[pl.ds(0, q_width), pl.ds(0, d)], local.at[spare])
    fetch.start()
    fetch.wait()

    def out_proj(t):
        c0 = at128(t, 512)
        mid_ref[:, pl.ds(c0, 512)] = (
            dot(o_ref[...], stage[pl.ds(0, q_width), pl.ds(c0, 512)]) + x_ref[:, pl.ds(c0, 512)].astype(F32)
        )

    loop(d // 512, out_proj)
    mid = mid_ref[...]
    inverse_two = lax.rsqrt(jnp.mean(mid * mid, -1, keepdims=True) + EPSILON)
    x_all[pl.ds(at128(z, rows), rows), :] = (mid * inverse_two * gain_ref[1:2, :]).astype(BF)
    c_x.begin()
    c_g.forward(nz - 1)
    for k in range(1, nz - 1):
        c_x.forward(k)
    p_gu.middle()
    if nz <= 4:
        c_x.forward(nz - 1)
    p_gu.late()
    p_d.begin()
    p_gu.finish()

    cols = 768 if wide % 768 == 0 else 256

    def hidden(j):
        r0 = at128(j, rows)

        def one(t):
            c0 = at128(t, cols)
            xb = x_all[pl.ds(r0, rows), :]
            gate = dot(xb, gu[:, pl.ds(c0, cols)])
            up = dot(xb, gu[:, pl.ds(pl.multiple_of(wide + c0, 128), cols)])
            act[pl.ds(r0, rows), pl.ds(c0, cols)] = (gate * jax.nn.sigmoid(gate) * up).astype(BF)
            dgu[pl.ds(r0, rows), pl.ds(c0, cols)] = gate.astype(BF)
            dgu[pl.ds(r0, rows), pl.ds(pl.multiple_of(wide + c0, 128), cols)] = up.astype(BF)

        loop(wide // cols, one)

    hidden(z)
    if nz > 4:
        c_x.forward(nz - 1)

    def nearest(k):
        c_x.arrive(k)
        hidden(c_x.order(k))

    loop(nz - 2, lambda i: nearest(i + 1))
    p_d.middle()
    nearest(nz - 1)
    for k in range(1, nz):
        c_g.arrive(k)
    high = 768 if nz <= 4 and wide % 768 == 0 else 256
    spots = [(r, c) for r in range(0, wide, high) for c in range(0, d, 768)]
    puts = []
    for i, (r, c) in enumerate(spots):
        if i >= 2:
            puts[i - 2].wait()
        slot = pl.ds(i % 2 * 768, 768)
        ybuf[0:high, slot] = dot_at(act[:, r : r + high], g_all[:, c : c + 768]).astype(BF)
        puts.append(
            pltpu.make_async_copy(
                ybuf.at[pl.ds(0, high), slot], dwd.at[pl.ds(r, high), pl.ds(c, 768)],
                local.at[spare + i % 2],
            )
        )
        puts[i].start()
        if i == len(spots) // 2:
            p_d.late()
    for put in puts[-2:]:
        put.wait()
    s_d.swap()
    p_d.finish()

    def back(j):
        r0 = at128(j, rows)

        def one(t):
            c0 = at128(t, cols)
            c1 = pl.multiple_of(wide + c0, 128)
            da = dot_bt(g_all[pl.ds(r0, rows), :], dnb[pl.ds(c0, cols), :])
            gate = dgu[pl.ds(r0, rows), pl.ds(c0, cols)].astype(F32)
            up = dgu[pl.ds(r0, rows), pl.ds(c1, cols)].astype(F32)
            sig = jax.nn.sigmoid(gate)
            dgu[pl.ds(r0, rows), pl.ds(c0, cols)] = (
                da * up * (sig * (1.0 + gate * (1.0 - sig)))
            ).astype(BF)
            dgu[pl.ds(r0, rows), pl.ds(c1, cols)] = (da * gate * sig).astype(BF)

        loop(wide // cols, one)

    rs = base

    slots = stage.at[:, pl.ds(0, d)]

    def slot_copy(src, dst, step):
        return remote(
            rows_at(slots, src, rows), rows_at(slots, dst, rows),
            send.at[rs + src], recv.at[rs + dst], z + step, me,
        )

    hold = nz <= 4

    def sides(i):
        j = c_x.order(nz - 1 - i)
        below, above = j > z, j < z
        got = jnp.logical_or(jnp.logical_and(below, z > 0), jnp.logical_and(above, z < nz - 1))
        return j, below, above, got, (pl.ds(at128(j, rows), rows), pl.ds(0, d))

    def terms(i, at):
        j = sides(i)[0]
        back(j)

        def one(t):
            c0 = at128(t, 768)
            ybuf[at : at + rows, pl.ds(c0, 768)] = dot_bt(
                dgu[pl.ds(at128(j, rows), rows), :], gu[pl.ds(c0, 768), :]
            ).astype(BF)

        loop(d // 768, one)

    def ship(j, below, above):
        @pl.when(below)
        def _():
            slot_copy(j, j, 1).start()

        @pl.when(above)
        def _():
            slot_copy(j, jnp.where(z - 1 == j, nz, j), -1).start()

    def early(i, at):
        j, below, above, got, where = sides(i)

        @pl.when(jnp.logical_not(got))
        def _():
            stage[where] = ybuf[at : at + rows, :]
            ship(j, below, above)

    def late(i, at):
        j, below, above, got, where = sides(i)

        @pl.when(got)
        def _():
            slot_copy(j, j, 0).wait_recv()
            stage[where] = (
                stage[where].astype(F32) + ybuf[at : at + rows, :].astype(F32)
            ).astype(BF)
            ship(j, below, above)

    if hold:
        between = {max(nz - 3, 0): (s_d.merge, s_d.first)}
        for i in range(nz - 1):
            terms(i, i * rows)
            early(i, i * rows)
            for step in between.get(i, ()):
                step()
        late(0, 0)
    else:

        def at_once(i):
            terms(i, 0)
            early(i, 0)
            late(i, 0)

        loop(nz - 1, at_once)
        for step in (s_d.merge, s_d.first, s_d.second):
            step()
    back(z)

    def own(t):
        c0 = at128(t, 512)
        dx_ref[:, pl.ds(c0, 512)] = dot_bt(
            dgu[pl.ds(at128(z, rows), rows), :], gu[pl.ds(c0, 512), :]
        )

    loop(d // 512, own)

    c_x.drain()

    def down_terms(t):
        c0 = at128(t, 512)
        g_all[:, pl.ds(c0, 512)] = dot(act[...], dnb[:, pl.ds(c0, 512)]).astype(BF)

    c_g.drain()
    loop(d // 512, down_terms)
    out_p = pltpu.make_async_copy(g_all, dpart, local.at[spare + 3])
    out_p.start()
    if hold:
        s_d.second()
        for i in range(1, nz - 1):
            late(i, i * rows)
    p_gu.drain()

    side = 768 if wide % 768 == 0 else 256

    def w_gu_grad(t):
        c0 = at128(t, side)
        for r in range(0, d, 768):
            gu[r : r + 768, pl.ds(c0, side)] = dot_at(
                x_all[:, r : r + 768], dgu[:, pl.ds(c0, side)]
            ).astype(BF)

    outs = []
    for i in range(2):
        loop(wide // side, lambda t: w_gu_grad(t + i * (wide // side)))
        half = pl.ds(i * wide, wide)
        outs.append(pltpu.make_async_copy(gu.at[:, half], dwgu.at[:, half], local.at[spare + i]))
        outs[-1].start()
    s_d.last(d_own)
    out_kv = pltpu.make_async_copy(kv, kv_out, local.at[spare + 2])
    out_kv.start()

    @pl.when(z > 0)
    def _():
        slot_copy(z, z, 0).wait_recv()
        dx_ref[...] += rows_at(slots, z, rows)[...].astype(F32)

    @pl.when(z < nz - 1)
    def _():
        slot_copy(z, nz, 0).wait_recv()
        dx_ref[...] += rows_at(slots, nz, rows)[...].astype(F32)

    for item in (p_q, p_kv, p_s, p_o, p_d, c_kv, s_d):
        item.drain()

    def gave(i):
        j = c_x.order(i + 1)
        slot_copy(j, j, 0).wait_send()

    loop(nz - 1, gave)
    for copy in outs + [out_kv, out_p]:
        copy.wait()


def front(dims, wq, sm, wo, w_gu, w_dn, x, g, cos2, sin2, qpos, kpos):
    nz, nf, rows, d, ff, wide, upad, nb, ng = dims
    q_width, k_width = HEADS * HEAD_DIM, KV_HEADS * HEAD_DIM
    qkv = q_width + 2 * k_width
    tokens = nz * rows
    any_, vm = pl.BlockSpec(memory_space=pl.ANY), pl.BlockSpec(memory_space=pltpu.VMEM)
    sems = 6 * PlaneGather.sems(nf) + 3 * Chain.sems(nz) + Scatter.sems(nf) + nz + 1
    chips = nf // 2
    out = jax.ShapeDtypeStruct
    return pl.pallas_call(
        functools.partial(front_kernel, dims),
        in_specs=[any_] * 5 + [vm, any_] + [vm] * 4,
        out_specs=[any_, any_, vm, any_] + [vm] * 5 + [any_] * 6,
        out_shape=[
            out((d, qkv), BF),
            out((q_width, d), BF),
            out((rows, q_width), BF),
            out((tokens, 2 * k_width), BF),
            out((rows, q_width), BF),
            out((rows, HEAD_DIM), F32),
            out((rows, d), F32),
            out((rows, d), F32),
            out((8, d), F32),
            out((d, 2 * wide), BF),
            out((tokens, d), BF),
            out((upad, d), BF),
            out((wide, d), BF),
            out((chips * upad, d), BF),
            out(((chips - 1) * upad, d), BF),
        ],
        scratch_shapes=[
            pltpu.VMEM((max(d, (nz + 1) * rows), qkv), BF),
            pltpu.VMEM((d, 2 * wide), BF),
            pltpu.VMEM((wide, d), BF),
            pltpu.VMEM((tokens, d), BF),
            pltpu.VMEM((tokens, d), BF),
            pltpu.VMEM((tokens, wide), BF),
            pltpu.VMEM((tokens, 2 * wide), BF),
            pltpu.VMEM((nf * 16, sm.shape[1]), BF),
            pltpu.VMEM((tokens, 2 * k_width), BF),
            pltpu.VMEM((8, qkv), F32),
            pltpu.VMEM(((nz - 1 if nz <= 4 else 1) * rows, d), BF),
            pltpu.VMEM((d // nf, 2 * wide), BF),
            pltpu.VMEM((upad, d), BF),
            pltpu.SemaphoreType.DMA((sems,)),
            pltpu.SemaphoreType.DMA((sems,)),
            pltpu.SemaphoreType.DMA((24,)),
        ],
        compiler_params=pltpu.CompilerParams(
            collective_id=0, has_side_effects=True, vmem_limit_bytes=VMEM_LIMIT
        ),
    )(wq, sm, wo, w_gu, w_dn, x, g, cos2, sin2, qpos, kpos)


class Reduce:
    def __init__(self, slots, rows, nz, z, me, send, recv, base, order):
        self.slots, self.rows, self.nz, self.z, self.me = slots, rows, nz, z, me
        self.send, self.recv, self.base, self.order = send, recv, base, order

    @staticmethod
    def sems(nz):
        return nz + 1

    def copy(self, src, dst, step):
        return remote(
            rows_at(self.slots, src, self.rows), rows_at(self.slots, dst, self.rows),
            self.send.at[self.base + src], self.recv.at[self.base + dst], self.z + step, self.me,
        )

    def give(self, i, part):
        z, nz, rows = self.z, self.nz, self.rows
        j = self.order(nz - 1 - i)
        below, above = j > z, j < z
        got = jnp.logical_or(jnp.logical_and(below, z > 0), jnp.logical_and(above, z < nz - 1))
        where = pl.ds(at128(j, rows) if rows % 128 == 0 else pl.multiple_of(j * rows, 16), rows)
        own = part(j)

        @pl.when(got)
        def _():
            self.copy(j, j, 0).wait_recv()
            self.slots[where, :] = (self.slots[where, :].astype(F32) + own.astype(F32)).astype(BF)

        @pl.when(jnp.logical_not(got))
        def _():
            self.slots[where, :] = own.astype(BF)

        @pl.when(below)
        def _():
            self.copy(j, j, 1).start()

        @pl.when(above)
        def _():
            self.copy(j, jnp.where(z - 1 == j, nz, j), -1).start()

    def take(self, total):
        z, nz = self.z, self.nz

        @pl.when(z > 0)
        def _():
            self.copy(z, z, 0).wait_recv()
            total[...] += rows_at(self.slots, z, self.rows)[...].astype(F32)

        @pl.when(z < nz - 1)
        def _():
            self.copy(z, nz, 0).wait_recv()
            total[...] += rows_at(self.slots, nz, self.rows)[...].astype(F32)

    def drain(self):
        def gave(i):
            j = self.order(i + 1)
            self.copy(j, j, 0).wait_send()

        loop(self.nz - 1, gave)


def back_kernel(
    dims,
    dwgu, d_own, dpart, wq_all, wo_all, kv_hbm, mid_hbm, dx_hbm,
    x_ref, g_ref, q_ref, o_ref, lse_ref, gain_ref, cos_ref, sin_ref, qpos_ref, kpos_ref,
    hid_ref, gh_ref, all_d, all_g, all_u, z_out, tiny_out,
    stage, full, dslots, do_ref, kv, dkv, kslots, m32, dh, t32, dqkv, normed,
    r3, l3, r4, l4, zsrc, zslots, zlow, zown, gain_sums, tiny, tin, zin,
    r1, r2, l1, l2, own2, own_sems, send, recv, local,
):
    nz, nf, rows, d, wide, upad, nb, ng, ch = dims
    z, me = lax.axis_index("ctx"), lax.axis_index("fsdp")
    q_width, k_width = HEADS * HEAD_DIM, KV_HEADS * HEAD_DIM
    qkv = q_width + 2 * k_width
    scale = HEAD_DIM ** (-0.5)
    wr = d // nf
    place = {"nf": nf, "z": z, "me": me, "send": send, "recv": recv}
    per = Scatter.sems(nf)
    own = {"own": own2, "sems": own_sems}
    s_g = Scatter(dwgu, 0, wr, wide, r1, l1, True, base=per, **own, **place)
    s_u = Scatter(dwgu, wide, wr, wide, r2, l2, True, base=2 * per, **own, **place)
    s_o = Scatter(full, 0, wr, d, r3, l3, True, base=3 * per, **place)
    s_q = Scatter(full, 0, wr, qkv, r4, l4, True, base=4 * per, **place)
    base = 5 * per
    line = {"nz": nz, "z": z, "me": me, "send": send, "recv": recv}
    per = Chain.sems(nz)
    a_d = Chain(all_d, upad, base=base, **line)
    a_g = Chain(all_g, wr, base=base + per, **line)
    a_u = Chain(all_u, wr, base=base + 2 * per, **line)
    a_z = Chain(z_out, ch, base=base + 3 * per, **line)
    base += 4 * per
    per = Reduce.sems(nz)
    d_kv = Reduce(kslots, rows, base=base, order=a_d.order, **line)
    d_h = Reduce(dslots, rows, base=base + per, order=a_d.order, **line)
    d_z = Reduce(zslots, ch, base=base + 2 * per, order=a_d.order, **line)
    base += 3 * per

    def fetch(src, dst, i):
        copy = pltpu.make_async_copy(src, dst, local.at[i])
        copy.start()
        return copy

    def stream(src, cols, use):
        copies = []
        for t in range(src.shape[0] // 512):
            slot = stage.at[pl.ds(t % 2 * 512, 512), pl.ds(0, cols)]
            copies.append(
                pltpu.make_async_copy(src.at[pl.ds(t * 512, 512)], slot, local.at[6 + t % 2])
            )
        for copy in copies[:2]:
            copy.start()
        for t, copy in enumerate(copies):
            copy.wait()
            use(t, t % 2 * 512)
            if t + 2 < len(copies):
                copies[t + 2].start()

    mid_in = fetch(mid_hbm, m32, 1)
    dx_in = fetch(dx_hbm, dh, 2)
    kv_in = fetch(kv_hbm, kv, 3)
    d_in = fetch(d_own, rows_at(all_d, z, upad), 8)

    barrier = pltpu.get_barrier_semaphore()
    for k in range(1, nf):
        pl.semaphore_signal(barrier, inc=1, device_id=(z, me ^ k), device_id_type=MESH)
    for k in range(1, nz):
        pl.semaphore_signal(barrier, inc=1, device_id=((z + k) % nz, me), device_id_type=MESH)
    pl.semaphore_wait(barrier, nf + nz - 2)

    dkv[...] = jnp.zeros_like(dkv)
    lanes = lax.broadcasted_iota(jnp.int32, (rows, HEAD_DIM), 1)
    mine = dkv.at[pl.ds(at128(z, rows), rows)]
    third = HEADS // 3

    def norm_back():
        mid_in.wait()
        dx_in.wait()
        mid, dxn = m32[...], dh[...]
        inverse_two = lax.rsqrt(jnp.mean(mid * mid, -1, keepdims=True) + EPSILON)
        scaled = gain_ref[1:2, :] * dxn
        gain_sums[1:2, :] = jnp.sum(dxn * mid * inverse_two, 0, keepdims=True)
        dh[...] = (
            g_ref[...].astype(F32)
            + inverse_two * scaled
            - mid
            * (inverse_two * inverse_two * inverse_two)
            * jnp.mean(scaled * mid, -1, keepdims=True)
        )
        normed[...] = dh[...].astype(BF)

    def out_back():
        def one(t, r):
            do_ref[:, t * 512 : t * 512 + 512] = dot_bt(
                normed[...], stage[r : r + 512, 0:d]
            ).astype(BF)

        stream(wo_all, d, one)
        kv_in.wait()

    def w_out_grad():
        def one(t):
            c0 = at128(t, 512)
            full[pl.ds(0, q_width), pl.ds(c0, 512)] = dot_at(
                o_ref[...], normed[:, pl.ds(c0, 512)]
            ).astype(BF)

        loop(d // 512, one)

    def head(h):
        c0 = at128(h, HEAD_DIM)
        kc = at128(h // (HEADS // KV_HEADS), HEAD_DIM)
        vc = pl.multiple_of(kc + k_width, HEAD_DIM)
        q, k, v = q_ref[:, pl.ds(c0, HEAD_DIM)], kv[:, pl.ds(kc, HEAD_DIM)], kv[:, pl.ds(vc, HEAD_DIM)]
        do = do_ref[:, pl.ds(c0, HEAD_DIM)]
        lse = jnp.sum(jnp.where(lanes == h, lse_ref[...], 0.0), -1, keepdims=True)
        delta = jnp.sum(
            do.astype(F32) * o_ref[:, pl.ds(c0, HEAD_DIM)].astype(F32), -1, keepdims=True
        )
        s = jnp.where(kpos_ref[...] <= qpos_ref[...], dot_bt(q, k) * scale, MASKED)
        p = jnp.exp(s - lse)
        dkv[:, pl.ds(vc, HEAD_DIM)] += dot_at(p.astype(BF), do)
        ds = (p * (dot_bt(do, v) - delta)).astype(BF)
        dq = dot(ds, k) * scale
        dkv[:, pl.ds(kc, HEAD_DIM)] += dot_at(ds, q) * scale
        dqkv[:, pl.ds(c0, HEAD_DIM)] = turn(dq, cos_ref[...], -sin_ref[...]).astype(BF)

    def kv_part(j):
        return dkv[pl.ds(at128(j, rows), rows), :]

    def down_part(j):
        part = stage.at[pl.ds(0, rows), pl.ds(0, d)]
        fetch(rows_at(dpart, j, rows), part, 1).wait()
        return part[...]

    def z_part(j):
        return zsrc[pl.ds(pl.multiple_of(j * ch, 16), ch), :]

    def project_back():
        for h in range(KV_HEADS):
            c0 = h * HEAD_DIM
            dqkv[:, q_width + c0 : q_width + c0 + HEAD_DIM] = turn(
                mine[:, c0 : c0 + HEAD_DIM], cos_ref[...], -sin_ref[...]
            ).astype(BF)
        dqkv[:, q_width + k_width :] = mine[:, k_width:].astype(BF)

    def w_qkv_grad():
        x = x_ref[...].astype(F32)
        inverse = lax.rsqrt(jnp.mean(x * x, -1, keepdims=True) + EPSILON)
        normed[...] = (x * inverse * gain_ref[0:1, :]).astype(BF)
        s_o.drain()

        def one(t):
            c0 = at128(t, 512)
            full[pl.ds(0, d), pl.ds(c0, 512)] = dot_at(
                normed[...], dqkv[:, pl.ds(c0, 512)]
            ).astype(BF)

        loop(qkv // 512, one)

    tiny_copies = []

    def input_back():
        def one(t, r):
            t32[:, t * 512 : t * 512 + 512] = dot_bt(dqkv[...], stage[r : r + 512, :])

        stream(wq_all, qkv, one)
        x = x_ref[...].astype(F32)
        inverse = lax.rsqrt(jnp.mean(x * x, -1, keepdims=True) + EPSILON)
        dxn = t32[...]
        scaled = gain_ref[0:1, :] * dxn
        gain_one = jnp.sum(dxn * x * inverse, 0, keepdims=True)
        gain_two = gain_sums[1:2, :]
        bias = jnp.sum(dqkv[...].astype(F32), 0, keepdims=True)
        gh_ref[...] = (
            dh[...]
            + inverse * scaled
            - x * (inverse * inverse * inverse) * jnp.mean(scaled * x, -1, keepdims=True)
        ).astype(BF)

        cut = q_width + k_width
        qk, vb = cut // nf, k_width // nf
        tiny[...] = jnp.zeros_like(tiny)
        for f in range(nf):
            r = slice(8 * f, 8 * f + 1)
            tiny[r, 0:qk] = bias[:, f * qk : (f + 1) * qk]
            tiny[r, qk : qk + vb] = bias[:, cut + f * vb : cut + (f + 1) * vb]
            tiny[r, qk + vb : qk + vb + ng] = gain_one[:, f * ng : (f + 1) * ng]
            tiny[r, qk + vb + ng : qk + vb + 2 * ng] = gain_two[:, f * ng : (f + 1) * ng]
        own = pl.ds(pl.multiple_of(me * 8, 8), 8)
        tin[own, :] = tiny[own, :]
        for k in range(1, nf):
            copy = remote(
                rows_at(tiny, me ^ k, 8), rows_at(tin, me, 8),
                send.at[base + k], recv.at[base + k], z, me ^ k,
            )
            copy.start()
            tiny_copies.append(copy)

    def tiny_along():
        for copy in tiny_copies:
            copy.wait_recv()
        total = tin[0:8, :]
        for f in range(1, nf):
            total = total + tin[8 * f : 8 * f + 8, :]
        zin[pl.ds(pl.multiple_of(z * 8, 8), 8), :] = total
        for k in range(1, nz):
            copy = remote(
                rows_at(zin, z, 8), rows_at(zin, z, 8),
                send.at[base + nf + k], recv.at[base + nf + k], (z + k) % nz, me,
            )
            copy.start()
            tiny_copies.append(copy)

    def z_take():
        zown[...] = z_part(z).astype(F32)
        d_z.take(zown)
        zlow[...] = zown[...].astype(BF)
        fetch(zlow, rows_at(z_out, z, ch), 2).wait()

    def h_take():
        m32[...] += down_part(z).astype(F32)
        d_h.take(m32)
        hid_ref[...] = m32[...].astype(BF)

    a_d.begin(d_own)
    s_g.swap()
    norm_back()
    out_back()
    w_out_grad()
    s_o.swap()
    s_g.merge()
    s_g.first()
    s_u.swap()
    a_d.forward(1)
    for k in range(2, nz - 1):
        a_d.forward(k)
    loop(third, head)
    loop(third, lambda h: head(h + third))
    loop(third, lambda h: head(h + 2 * third))
    s_u.merge()
    s_g.second()
    s_u.first()
    a_d.forward(nz - 1)
    d_kv.give(0, kv_part)
    for i in range(1, nz - 2):
        d_kv.give(i, kv_part)
    d_kv.give(nz - 2, kv_part)
    s_o.merge()
    s_o.first()
    s_g.last(s_g.block(0))
    fetch(s_g.block(0), rows_at(all_g, z, wr), 4).wait()
    a_g.begin()
    s_u.second()
    a_g.forward(1)
    for k in range(2, nz - 1):
        a_g.forward(k)
    s_o.second()
    d_kv.take(mine)
    d_h.give(0, down_part)
    project_back()
    a_g.forward(nz - 1)
    w_qkv_grad()
    s_q.swap()
    s_o.last(zsrc.at[pl.ds(0, wr), pl.ds(0, d)])
    s_u.last(s_u.block(0))
    fetch(s_u.block(0), rows_at(all_u, z, wr), 5).wait()
    s_q.merge()
    s_q.first()
    a_u.begin()
    a_u.forward(1)
    s_q.second()
    for k in range(2, nz - 1):
        a_u.forward(k)
    a_u.forward(nz - 1)
    input_back()
    s_q.last(zsrc.at[pl.ds(0, wr), pl.ds(d, qkv)])
    d_z.give(0, z_part)
    tiny_along()
    for i in range(1, nz - 2):
        d_z.give(i, z_part)
    for i in range(1, nz - 2):
        d_h.give(i, down_part)
    d_z.give(nz - 2, z_part)
    d_h.give(nz - 2, down_part)
    for k in range(1, nz):
        a_u.arrive(k)
    z_take()
    for k in range(1, nz):
        a_g.arrive(k)
    a_z.begin()
    a_z.forward(1)
    for k in range(1, nz):
        a_d.arrive(k)
    for k in range(2, nz - 1):
        a_z.forward(k)
    a_z.forward(nz - 1)
    h_take()
    for k in range(1, nz):
        a_z.arrive(k)
    for copy in tiny_copies[nf - 1 :]:
        copy.wait_recv()
    total = zin[0:8, :]
    for j in range(1, nz):
        total = total + zin[8 * j : 8 * j + 8, :]
    tiny_out[...] = total
    d_in.wait()
    for item in (s_g, s_u, s_o, s_q, a_d, a_g, a_u, a_z, d_kv, d_h, d_z):
        item.drain()
    for copy in tiny_copies:
        copy.wait_send()


def back(dims, *args):
    nz, nf, rows, d, wide, upad, nb, ng, ch = dims
    q_width, k_width = HEADS * HEAD_DIM, KV_HEADS * HEAD_DIM
    qkv = q_width + 2 * k_width
    tokens, chips, wr = nz * rows, nf // 2, d // nf
    tiny = -(-((qkv + 2 * d) // nf) // 128) * 128
    any_, vm = pl.BlockSpec(memory_space=pl.ANY), pl.BlockSpec(memory_space=pltpu.VMEM)
    out = jax.ShapeDtypeStruct
    sems = 5 * Scatter.sems(nf) + 4 * Chain.sems(nz) + 3 * Reduce.sems(nz) + nf + nz
    pieces = [(upad, d), (wr, wide), (wr, wide)]
    return pl.pallas_call(
        functools.partial(back_kernel, dims),
        in_specs=[any_] * 8 + [vm] * 10,
        out_specs=[vm, vm] + [any_] * 4 + [vm],
        out_shape=[out((rows, d), BF), out((rows, d), BF)]
        + [out((nz * r, c), BF) for r, c in pieces]
        + [out((nz * ch, d + qkv), BF), out((8, tiny), F32)],
        scratch_shapes=[
            pltpu.VMEM((1024, qkv), BF),
            pltpu.VMEM((d, qkv), BF),
            pltpu.VMEM(((nz + 1) * rows, d), BF),
            pltpu.VMEM((rows, q_width), BF),
            pltpu.VMEM((tokens, 2 * k_width), BF),
            pltpu.VMEM((tokens, 2 * k_width), F32),
            pltpu.VMEM(((nz + 1) * rows, 2 * k_width), BF),
            pltpu.VMEM((rows, d), F32),
            pltpu.VMEM((rows, d), F32),
            pltpu.VMEM((rows, d), F32),
            pltpu.VMEM((rows, qkv), BF),
            pltpu.VMEM((rows, d), BF),
            pltpu.VMEM((chips * wr, d), BF),
            pltpu.VMEM(((chips - 1) * wr, d), BF),
            pltpu.VMEM((chips * wr, qkv), BF),
            pltpu.VMEM(((chips - 1) * wr, qkv), BF),
            pltpu.VMEM((nz * ch, d + qkv), BF),
            pltpu.VMEM(((nz + 1) * ch, d + qkv), BF),
            pltpu.VMEM((ch, d + qkv), BF),
            pltpu.VMEM((ch, d + qkv), F32),
            pltpu.VMEM((8, d), F32),
            pltpu.VMEM((nf * 8, tiny), F32),
            pltpu.VMEM((nf * 8, tiny), F32),
            pltpu.VMEM((nz * 8, tiny), F32),
            pltpu.VMEM((chips * wr, wide), BF),
            pltpu.VMEM((chips * wr, wide), BF),
            pltpu.VMEM(((chips - 1) * wr, wide), BF),
            pltpu.VMEM(((chips - 1) * wr, wide), BF),
            pltpu.VMEM((2 * wr, wide), BF),
            pltpu.SemaphoreType.DMA((2,)),
            pltpu.SemaphoreType.DMA((sems,)),
            pltpu.SemaphoreType.DMA((sems,)),
            pltpu.SemaphoreType.DMA((9,)),
        ],
        compiler_params=pltpu.CompilerParams(
            collective_id=1, has_side_effects=True, vmem_limit_bytes=VMEM_LIMIT
        ),
    )(*args)


def shards(
    hidden_in, w_qkv, b_qkv, w_out, w_gate_up, w_down, gain_attn, gain_mlp, block_order, cotangent
):
    nz, nf = lax.axis_size("ctx"), lax.axis_size("fsdp")
    z, me = lax.axis_index("ctx"), lax.axis_index("fsdp")
    q_width, k_width = HEADS * HEAD_DIM, KV_HEADS * HEAD_DIM
    rows = hidden_in.shape[1]
    piece_len = rows // 2
    ff = w_gate_up.shape[1] // 2
    unit = ff // (nf * nz)
    order_row = block_order[0]
    all_places = (
        order_row[:, None] * piece_len + jnp.arange(piece_len, dtype=jnp.int32)[None, :]
    ).reshape(-1)
    my_places = lax.dynamic_slice_in_dim(all_places, z * rows, rows)
    cosine, sine_table = angle_tables(my_places)
    cos2 = jnp.concatenate([cosine, cosine], 1)
    sin2 = jnp.concatenate([-sine_table, sine_table], 1)

    upad = -(-unit // 16) * 16
    wide = nf * upad
    nb, ng = b_qkv.shape[0], gain_attn.shape[0]
    d = hidden_in.shape[2]
    small = jnp.concatenate([b_qkv, gain_attn, gain_mlp])
    small = jnp.pad(small[None], ((0, 15), (0, -small.shape[0] % 128)))
    grad_low = cotangent[0]
    (whole_qkv, whole_out, q_low, kv_all, attn_low, lse, middle, grad_normed_two, gains, gate_up_local, down_part,
     down_own, *_) = front(
        (nz, nf, rows, d, ff, wide, upad, nb, ng),
        w_qkv, small, w_out, w_gate_up, w_down, hidden_in[0], grad_low, cos2, sin2,
        my_places[:, None], all_places[None, :],
    )
    ch = -(-(d // (nf * nz)) // 16) * 16
    hidden, grad_hidden, down_all, gate_all, up_all, attn_all, tiny = back(
        (nz, nf, rows, d, wide, upad, nb, ng, ch),
        gate_up_local, down_own, down_part, whole_qkv, whole_out, kv_all, middle, grad_normed_two,
        hidden_in[0], grad_low, q_low, attn_low, lse, gains, cos2, sin2, my_places[:, None], all_places[None, :],
    )
    e1 = (q_width + k_width) // nf
    e2 = e1 + k_width // nf
    e3 = e2 + ng
    shard = d // nf
    cuts = (0, e1, e2, e3, e3 + ng)
    if unit % 8 == 0 and shard % (16 * nz) == 0 and ch * nz == shard:
        gu_grad, down_grad, qkv_grad, out_grad, hidden, grad_hidden, *smalls = finish(
            gate_all, up_all, down_all, attn_all, tiny, hidden, grad_hidden, nz, nf, ff, cuts
        )
        b_qk, b_v, g_one, g_two = (item[0] for item in smalls)
    else:
        gu_grad = unpack(gate_all, up_all, nz, nf, ff)
        down_grad = down_all.reshape(nz, upad, d)[:, :unit].reshape(nz * unit, d).astype(F32)
        qkv_grad = attn_all[:shard, d:].astype(F32)
        out_grad = attn_all[:shard, :d].astype(F32)
        b_qk, b_v, g_one, g_two = (tiny[0, lo:hi] for lo, hi in zip(cuts, cuts[1:]))
    return (
        hidden[None],
        grad_hidden[None],
        qkv_grad,
        b_qk,
        b_v,
        out_grad,
        gu_grad,
        down_grad,
        g_one,
        g_two,
    )


def solution(mesh):
    placed = (
        P("fsdp", "ctx", None),
        P("fsdp", None),
        P("fsdp"),
        P("fsdp", None),
        P("fsdp", None),
        P("fsdp", None),
        P("fsdp"),
        P("fsdp"),
        P("fsdp", None),
        P("fsdp", "ctx", None),
    )
    return jax.shard_map(
        shards,
        mesh=mesh,
        in_specs=placed,
        out_specs=(
            P("fsdp", "ctx", None),
            P("fsdp", "ctx", None),
            P("fsdp", None),
            P("fsdp"),
            P("fsdp"),
            P("fsdp", None),
            P("fsdp", None),
            P("fsdp", None),
            P("fsdp"),
            P("fsdp"),
        ),
        check_vma=False,
    )
```

profile of v0, /device:TPU:0, one launch (start us, length us, event | category | flops | bytes accessed | tf_op | source)
XLA Modules:
  0.0 482.4 jit_solution(14614333946492294885)
XLA Ops:
  0.6 0.7 multiply_bitcast_fusion
  1.3 0.8 pad_maximum_fusion.2
  2.1 0.7 iota_add_fusion
  2.7 0.1 fusion.2
  2.8 0.6 pad.4.sm
  3.4 0.8 copy.20.qpos_ref
  4.2 0.5 fusion
  4.8 0.8 pad_maximum_fusion
  5.6 225.2 %shard_map.177 = (bf16[1536,2048]{1,0:T(8,128)(2,1)}, bf16[1536,1536]{1,0:T(8,128)(2,1)}, bf16[256,1536]{1,0:T(8,128)(2,1)}, bf16[1024,512]{1,0:T(8,128)(2,1)}, ...) custom-call(bf16[192,2048]{1,0:T(8,128)(2,1)} %wq.1, ...), custom_call_target="tpu_custom_call" | custom-call | tf_op jit(solution)/shard_map/pallas_call | solution.py:944
  230.8 236.9 %shard_map.178 = (bf16[256,1536]{1,0:T(8,128)(2,1)}, bf16[256,1536]{1,0:T(8,128)(2,1)}, bf16[1152,1536]{1,0:T(8,128)(2,1)}, bf16[768,2304]{1,0:T(8,128)(2,1)}, b...) custom-call(bf16[1536,4608]{1,0:T(8,128)(2,1)} %get-tuple-element.39.dwgu, ...), custom_call_target="tpu_custom_call" | custom-call | tf_op jit(solution)/shard_map/pallas_call | solution.py:1371
  467.7 14.3 %shard_map.179 = (f32[192,17920]{1,0:T(8,128)}, f32[1120,1536]{1,0:T(8,128)}, f32[192,2048]{1,0:T(8,128)}, f32[192,1536]{1,0:T(8,128)}, bf16[256,1536]{1,0:T(8,1...) custom-call(bf16[768,2304]{1,0:T(8,128)(2,1)} %get-tuple-element.51., ...), custom_call_target="tpu_custom_call" | custom-call | tf_op jit(solution)/shard_map/pallas_call | solution.py:128
  (2 shorter events, 0.0 us)
where the time goes:
time: 487 us; the launch traced here: 482 us
  Pallas kernels  476 us (98%)
    pallas_call x1, Pallas kernels, back(): pl.pallas_call(functools.partial(back_kernel, dims), in_specs=[any_] * 8...  237 us
    pallas_call x1, Pallas kernels, front(): pl.pallas_call(functools.partial(front_kernel, dims), in_specs=[any_] * 5...  225 us
    pallas_call x1, Pallas kernels, finish(): pl.pallas_call(functools.partial(finish_kernel, nz, nf, ff, unit, upad, c...  14.3 us

commit v1 on v0

--- a/solution.py
+++ b/solution.py
@@ -29,11 +29,17 @@
     return lax.dot_general(a, b, (((0,), (0,)), ((), ())), preferred_element_type=F32)
 
 
-def angle_tables(places):
-    half_dim = HEAD_DIM // 2
-    freqs = THETA ** (-(jnp.arange(half_dim).astype(F32) * 2.0 / HEAD_DIM))
-    angles = places.astype(F32)[:, None] * freqs[None, :]
-    return (jnp.cos(angles), jnp.sin(angles))
+def positions(order_ref, z, rows, tokens):
+    half = rows // 2
+    row = lax.broadcasted_iota(jnp.int32, (rows, 1), 0)
+    mine = jnp.where(
+        row < half, order_ref[0, 2 * z] * half + row, order_ref[0, 2 * z + 1] * half + row - half
+    )
+    lane = lax.broadcasted_iota(jnp.int32, (1, tokens), 1)
+    places = lane
+    for i in range(tokens // half):
+        places = jnp.where(lane >= i * half, order_ref[0, i] * half + lane - i * half, places)
+    return mine, places
 
 
 def half_rows(rows):
@@ -94,7 +100,7 @@
     down, attn, tiny, hid, gh = refs[2 * nz : 2 * nz + 5]
     gu_out, down_out, qkv_out, out_out, hid_out, gh_out, *tiny_outs = refs[2 * nz + 5 :]
     unpack_kernel(nz, nf, ff, unit, upad, *gates, *ups, gu_out)
-    down_out[...] = down[0:unit, :].astype(F32)
+    down_out[...] = down[...].astype(F32)[0:unit]
     d = out_out.shape[1]
     qkv_out[...] = attn[:, d:].astype(F32)
     out_out[...] = attn[:, :d].astype(F32)
@@ -397,10 +403,12 @@
         step = rows if rows <= 96 else rows // 2
         n = rows // step
         core, col = self.core, self.c0 // cols
-        own = pl.BlockSpec((step, cols), lambda p, i: ((2 * p + core) * n + i, col))
+        deep = {"pipeline_mode": pl.Buffered(3)}
+        own = pl.BlockSpec((step, cols), lambda p, i: ((2 * p + core) * n + i, col), **deep)
+        held_in = pl.BlockSpec((step, cols), lambda p, i: (p * n + i, 0), **deep)
         held = pl.BlockSpec((step, cols), lambda p, i: (p * n + i, 0))
         pltpu.emit_pipeline(
-            add_two, grid=(self.chips, n), in_specs=[own, held], out_specs=[held]
+            add_two, grid=(self.chips, n), in_specs=[own, held_in], out_specs=[held]
         )(self.src, self.recv4, self.recv4)
 
     def fetch(self, p):
@@ -418,7 +426,7 @@
                 total = total + part[...].astype(F32)
             out[...] = total.astype(BF)
             return
-        step = n if n <= 96 else n // 2
+        step = n // 2 if n % 32 == 0 and n > 144 else n
         spec = pl.BlockSpec((step, self.cols), lambda i: (i, 0))
         body = add_two if len(parts) == 2 else add_all
         pltpu.emit_pipeline(
@@ -518,8 +526,9 @@
 
 def front_kernel(
     dims,
-    wq, sm, wo, w_gu, w_dn, x_ref, g_ref, cos_ref, sin_ref, qpos_ref, kpos_ref,
-    wq_all, wo_all, q_ref, kv_out, o_ref, lse_ref, mid_ref, dx_ref, gain_ref, dwgu, dpart, d_own, dwd, r0, l0,
+    wq, sm, wo, w_gu, w_dn, x_ref, g_ref, order_ref, freq_ref,
+    wq_all, wo_all, q_out, kv_out, o_out, lse_out, mid_out, dx_ref, gain_out, cos_out, sin_out, dwgu, dpart, d_own, dwd, r0, l0,
+    q_ref, o_ref, lse_ref, mid_ref, gain_ref, cos_ref, sin_ref, qpos_ref, kpos_ref,
     stage, gu, dnb, g_all, x_all, act, dgu, smb, kv, bias, ybuf, packed, down, send, recv, local,
 ):
     nz, nf, rows, d, ff, wide, upad, nb, ng = dims
@@ -593,9 +602,9 @@
                 pack(k, nz, nf, ff, unit, upad, wr, width, dgu, packed)
                 copy, off = down_load(k)
                 copy.wait()
-                down[0:unit, :] = down_in[...].astype(F32)[off : off + unit].astype(BF)
-                if upad > unit:
-                    down[unit:upad, :] = jnp.zeros((upad - unit, d), BF)
+                part = down_in[...].astype(F32)[off : off + unit]
+                rest = jnp.zeros((upad - unit, d), F32)
+                down[...] = jnp.concatenate([part, rest], 0).astype(BF)
 
     g_copy = pltpu.make_async_copy(g_ref, rows_at(g_all, z, rows), local.at[spare])
     g_copy.start()
@@ -606,12 +615,28 @@
     c_g.begin()
     part_loads()
 
+    given = []
+
+    def give_out(src, dst):
+        copy = pltpu.make_async_copy(src, dst, local.at[spare + 16 + len(given)])
+        copy.start()
+        given.append(copy)
+
     x = x_ref[...].astype(F32)
     inverse = lax.rsqrt(jnp.mean(x * x, -1, keepdims=True) + EPSILON)
 
     p_s.middle()
     p_kv.middle()
     p_q.begin()
+    tokens = nz * rows
+    qpos_ref[...], kpos_ref[...] = positions(order_ref, z, rows, tokens)
+    angle = qpos_ref[...].astype(F32) * freq_ref[...]
+    cos_ref[...] = jnp.cos(angle)
+    first_half = lax.broadcasted_iota(jnp.int32, angle.shape, 1) < HEAD_DIM // 2
+    sine = jnp.sin(angle)
+    sin_ref[...] = jnp.where(first_half, -sine, sine)
+    give_out(cos_ref, cos_out)
+    give_out(sin_ref, sin_out)
     p_s.late()
     p_kv.late()
     p_s.finish()
@@ -620,6 +645,7 @@
         bias[0:1, f * nb : (f + 1) * nb] = row[:, :nb]
         gain_ref[0:1, f * ng : (f + 1) * ng] = row[:, nb : nb + ng]
         gain_ref[1:2, f * ng : (f + 1) * ng] = row[:, nb + ng : nb + 2 * ng]
+    give_out(gain_ref, gain_out)
     normed = (x * inverse * gain_ref[0:1, :]).astype(BF)
     x_all[pl.ds(at128(z, rows), rows), :] = normed
 
@@ -670,6 +696,7 @@
         q_ref[:, pl.ds(c0, 256)] = turned(y)
 
     loop(q_width // 256, project_q)
+    give_out(q_ref, q_out)
     p_o.middle()
     p_gu.begin()
     for k in range(1, nz):
@@ -694,6 +721,8 @@
         lse_ref[...] = jnp.where(lanes == h, top + jnp.log(total), lse_ref[...])
 
     loop(HEADS, head)
+    give_out(o_ref, o_out)
+    give_out(lse_ref, lse_out)
     p_o.late()
     p_o.finish()
     fetch = pltpu.make_async_copy(wo_all, stage.at[pl.ds(0, q_width), pl.ds(0, d)], local.at[spare])
@@ -707,6 +736,7 @@
         )
 
     loop(d // 512, out_proj)
+    give_out(mid_ref, mid_out)
     mid = mid_ref[...]
     inverse_two = lax.rsqrt(jnp.mean(mid * mid, -1, keepdims=True) + EPSILON)
     x_all[pl.ds(at128(z, rows), rows), :] = (mid * inverse_two * gain_ref[1:2, :]).astype(BF)
@@ -715,10 +745,10 @@
     for k in range(1, nz - 1):
         c_x.forward(k)
     p_gu.middle()
+    p_d.begin()
     if nz <= 4:
         c_x.forward(nz - 1)
     p_gu.late()
-    p_d.begin()
     p_gu.finish()
 
     cols = 768 if wide % 768 == 0 else 256
@@ -848,13 +878,14 @@
             ship(j, below, above)
 
     if hold:
-        between = {max(nz - 3, 0): (s_d.merge, s_d.first)}
+        between = {0: (s_d.merge, s_d.first)}
         for i in range(nz - 1):
             terms(i, i * rows)
             early(i, i * rows)
             for step in between.get(i, ()):
                 step()
         late(0, 0)
+        s_d.second()
     else:
 
         def at_once(i):
@@ -886,7 +917,6 @@
     out_p = pltpu.make_async_copy(g_all, dpart, local.at[spare + 3])
     out_p.start()
     if hold:
-        s_d.second()
         for i in range(1, nz - 1):
             late(i, i * rows)
     p_gu.drain()
@@ -928,11 +958,11 @@
         slot_copy(j, j, 0).wait_send()
 
     loop(nz - 1, gave)
-    for copy in outs + [out_kv, out_p]:
+    for copy in outs + given + [out_kv, out_p]:
         copy.wait()
 
 
-def front(dims, wq, sm, wo, w_gu, w_dn, x, g, cos2, sin2, qpos, kpos):
+def front(dims, wq, sm, wo, w_gu, w_dn, x, g, order, freq):
     nz, nf, rows, d, ff, wide, upad, nb, ng = dims
     q_width, k_width = HEADS * HEAD_DIM, KV_HEADS * HEAD_DIM
     qkv = q_width + 2 * k_width
@@ -943,8 +973,8 @@
     out = jax.ShapeDtypeStruct
     return pl.pallas_call(
         functools.partial(front_kernel, dims),
-        in_specs=[any_] * 5 + [vm, any_] + [vm] * 4,
-        out_specs=[any_, any_, vm, any_] + [vm] * 5 + [any_] * 6,
+        in_specs=[any_] * 5 + [vm, any_, pl.BlockSpec(memory_space=pltpu.SMEM), vm],
+        out_specs=[any_] * 7 + [vm] + [any_] * 9,
         out_shape=[
             out((d, qkv), BF),
             out((q_width, d), BF),
@@ -955,6 +985,8 @@
             out((rows, d), F32),
             out((rows, d), F32),
             out((8, d), F32),
+            out((rows, HEAD_DIM), F32),
+            out((rows, HEAD_DIM), F32),
             out((d, 2 * wide), BF),
             out((tokens, d), BF),
             out((upad, d), BF),
@@ -963,6 +995,15 @@
             out(((chips - 1) * upad, d), BF),
         ],
         scratch_shapes=[
+            pltpu.VMEM((rows, q_width), BF),
+            pltpu.VMEM((rows, q_width), BF),
+            pltpu.VMEM((rows, HEAD_DIM), F32),
+            pltpu.VMEM((rows, d), F32),
+            pltpu.VMEM((8, d), F32),
+            pltpu.VMEM((rows, HEAD_DIM), F32),
+            pltpu.VMEM((rows, HEAD_DIM), F32),
+            pltpu.VMEM((rows, 1), jnp.int32),
+            pltpu.VMEM((1, tokens), jnp.int32),
             pltpu.VMEM((max(d, (nz + 1) * rows), qkv), BF),
             pltpu.VMEM((d, 2 * wide), BF),
             pltpu.VMEM((wide, d), BF),
@@ -978,12 +1019,12 @@
             pltpu.VMEM((upad, d), BF),
             pltpu.SemaphoreType.DMA((sems,)),
             pltpu.SemaphoreType.DMA((sems,)),
-            pltpu.SemaphoreType.DMA((24,)),
+            pltpu.SemaphoreType.DMA((32,)),
         ],
         compiler_params=pltpu.CompilerParams(
             collective_id=0, has_side_effects=True, vmem_limit_bytes=VMEM_LIMIT
         ),
-    )(wq, sm, wo, w_gu, w_dn, x, g, cos2, sin2, qpos, kpos)
+    )(wq, sm, wo, w_gu, w_dn, x, g, order, freq)
 
 
 class Reduce:
@@ -1050,8 +1091,9 @@
 def back_kernel(
     dims,
     dwgu, d_own, dpart, wq_all, wo_all, kv_hbm, mid_hbm, dx_hbm,
+    x_hbm, g_hbm, q_hbm, o_hbm, lse_hbm, gain_hbm, cos_hbm, sin_hbm, order_ref,
+    hid_ref, gh_ref, all_d, all_g, all_u, z_out, tiny_out,
     x_ref, g_ref, q_ref, o_ref, lse_ref, gain_ref, cos_ref, sin_ref, qpos_ref, kpos_ref,
-    hid_ref, gh_ref, all_d, all_g, all_u, z_out, tiny_out,
     stage, full, dslots, do_ref, kv, dkv, kslots, m32, dh, t32, dqkv, normed,
     r3, l3, r4, l4, zsrc, zslots, zlow, zown, gain_sums, tiny, tin, zin,
     r1, r2, l1, l2, own2, own_sems, send, recv, local,
@@ -1103,9 +1145,23 @@
             if t + 2 < len(copies):
                 copies[t + 2].start()
 
-    mid_in = fetch(mid_hbm, m32, 1)
-    dx_in = fetch(dx_hbm, dh, 2)
-    kv_in = fetch(kv_hbm, kv, 3)
+    coming = {}
+
+    def bring(name, src, dst):
+        coming[name] = fetch(src, dst, 9 + len(coming))
+
+    def need(*names):
+        for name in names:
+            if name in coming:
+                coming.pop(name).wait()
+
+    arrays = (
+        ("mid", mid_hbm, m32), ("dx", dx_hbm, dh), ("g", g_hbm, g_ref), ("gain", gain_hbm, gain_ref),
+        ("o", o_hbm, o_ref), ("kv", kv_hbm, kv), ("q", q_hbm, q_ref), ("lse", lse_hbm, lse_ref),
+        ("cos", cos_hbm, cos_ref), ("sin", sin_hbm, sin_ref), ("x", x_hbm, x_ref),
+    )
+    for array in arrays:
+        bring(*array)
     d_in = fetch(d_own, rows_at(all_d, z, upad), 8)
 
     barrier = pltpu.get_barrier_semaphore()
@@ -1116,13 +1172,13 @@
     pl.semaphore_wait(barrier, nf + nz - 2)
 
     dkv[...] = jnp.zeros_like(dkv)
+    qpos_ref[...], kpos_ref[...] = positions(order_ref, z, rows, nz * rows)
     lanes = lax.broadcasted_iota(jnp.int32, (rows, HEAD_DIM), 1)
     mine = dkv.at[pl.ds(at128(z, rows), rows)]
     third = HEADS // 3
 
     def norm_back():
-        mid_in.wait()
-        dx_in.wait()
+        need("mid", "dx", "g", "gain")
         mid, dxn = m32[...], dh[...]
         inverse_two = lax.rsqrt(jnp.mean(mid * mid, -1, keepdims=True) + EPSILON)
         scaled = gain_ref[1:2, :] * dxn
@@ -1143,9 +1199,10 @@
             ).astype(BF)
 
         stream(wo_all, d, one)
-        kv_in.wait()
 
     def w_out_grad():
+        need("o")
+
         def one(t):
             c0 = at128(t, 512)
             full[pl.ds(0, q_width), pl.ds(c0, 512)] = dot_at(
@@ -1153,6 +1210,10 @@
             ).astype(BF)
 
         loop(d // 512, one)
+
+    def heads(start, count):
+        need("o", "kv", "q", "lse", "cos", "sin")
+        loop(count, lambda i: head(i + start))
 
     def head(h):
         c0 = at128(h, HEAD_DIM)
@@ -1192,6 +1253,7 @@
         dqkv[:, q_width + k_width :] = mine[:, k_width:].astype(BF)
 
     def w_qkv_grad():
+        need("x")
         x = x_ref[...].astype(F32)
         inverse = lax.rsqrt(jnp.mean(x * x, -1, keepdims=True) + EPSILON)
         normed[...] = (x * inverse * gain_ref[0:1, :]).astype(BF)
@@ -1282,9 +1344,9 @@
     a_d.forward(1)
     for k in range(2, nz - 1):
         a_d.forward(k)
-    loop(third, head)
-    loop(third, lambda h: head(h + third))
-    loop(third, lambda h: head(h + 2 * third))
+    heads(0, third)
+    heads(third, third)
+    heads(2 * third, third)
     s_u.merge()
     s_g.second()
     s_u.first()
@@ -1370,12 +1432,22 @@
     pieces = [(upad, d), (wr, wide), (wr, wide)]
     return pl.pallas_call(
         functools.partial(back_kernel, dims),
-        in_specs=[any_] * 8 + [vm] * 10,
+        in_specs=[any_] * 16 + [pl.BlockSpec(memory_space=pltpu.SMEM)],
         out_specs=[vm, vm] + [any_] * 4 + [vm],
         out_shape=[out((rows, d), BF), out((rows, d), BF)]
         + [out((nz * r, c), BF) for r, c in pieces]
         + [out((nz * ch, d + qkv), BF), out((8, tiny), F32)],
         scratch_shapes=[
+            pltpu.VMEM((rows, d), BF),
+            pltpu.VMEM((rows, d), BF),
+            pltpu.VMEM((rows, q_width), BF),
+            pltpu.VMEM((rows, q_width), BF),
+            pltpu.VMEM((rows, HEAD_DIM), F32),
+            pltpu.VMEM((8, d), F32),
+            pltpu.VMEM((rows, HEAD_DIM), F32),
+            pltpu.VMEM((rows, HEAD_DIM), F32),
+            pltpu.VMEM((rows, 1), jnp.int32),
+            pltpu.VMEM((1, tokens), jnp.int32),
             pltpu.VMEM((1024, qkv), BF),
             pltpu.VMEM((d, qkv), BF),
             pltpu.VMEM(((nz + 1) * rows, d), BF),
@@ -1408,7 +1480,7 @@
             pltpu.SemaphoreType.DMA((2,)),
             pltpu.SemaphoreType.DMA((sems,)),
             pltpu.SemaphoreType.DMA((sems,)),
-            pltpu.SemaphoreType.DMA((9,)),
+            pltpu.SemaphoreType.DMA((20,)),
         ],
         compiler_params=pltpu.CompilerParams(
             collective_id=1, has_side_effects=True, vmem_limit_bytes=VMEM_LIMIT
@@ -1420,21 +1492,12 @@
     hidden_in, w_qkv, b_qkv, w_out, w_gate_up, w_down, gain_attn, gain_mlp, block_order, cotangent
 ):
     nz, nf = lax.axis_size("ctx"), lax.axis_size("fsdp")
-    z, me = lax.axis_index("ctx"), lax.axis_index("fsdp")
     q_width, k_width = HEADS * HEAD_DIM, KV_HEADS * HEAD_DIM
     rows = hidden_in.shape[1]
-    piece_len = rows // 2
     ff = w_gate_up.shape[1] // 2
     unit = ff // (nf * nz)
-    order_row = block_order[0]
-    all_places = (
-        order_row[:, None] * piece_len + jnp.arange(piece_len, dtype=jnp.int32)[None, :]
-    ).reshape(-1)
-    my_places = lax.dynamic_slice_in_dim(all_places, z * rows, rows)
-    cosine, sine_table = angle_tables(my_places)
-    cos2 = jnp.concatenate([cosine, cosine], 1)
-    sin2 = jnp.concatenate([-sine_table, sine_table], 1)
-
+    freqs = THETA ** (-(jnp.arange(HEAD_DIM // 2).astype(F32) * 2.0 / HEAD_DIM))
+    freqs = jnp.concatenate([freqs, freqs])[None]
     upad = -(-unit // 16) * 16
     wide = nf * upad
     nb, ng = b_qkv.shape[0], gain_attn.shape[0]
@@ -1442,17 +1505,16 @@
     small = jnp.concatenate([b_qkv, gain_attn, gain_mlp])
     small = jnp.pad(small[None], ((0, 15), (0, -small.shape[0] % 128)))
     grad_low = cotangent[0]
-    (whole_qkv, whole_out, q_low, kv_all, attn_low, lse, middle, grad_normed_two, gains, gate_up_local, down_part,
+    (whole_qkv, whole_out, q_low, kv_all, attn_low, lse, middle, grad_normed_two, gains, cos2, sin2, gate_up_local, down_part,
      down_own, *_) = front(
         (nz, nf, rows, d, ff, wide, upad, nb, ng),
-        w_qkv, small, w_out, w_gate_up, w_down, hidden_in[0], grad_low, cos2, sin2,
-        my_places[:, None], all_places[None, :],
+        w_qkv, small, w_out, w_gate_up, w_down, hidden_in[0], grad_low, block_order, freqs,
     )
     ch = -(-(d // (nf * nz)) // 16) * 16
     hidden, grad_hidden, down_all, gate_all, up_all, attn_all, tiny = back(
         (nz, nf, rows, d, wide, upad, nb, ng, ch),
         gate_up_local, down_own, down_part, whole_qkv, whole_out, kv_all, middle, grad_normed_two,
-        hidden_in[0], grad_low, q_low, attn_low, lse, gains, cos2, sin2, my_places[:, None], all_places[None, :],
+        hidden_in[0], grad_low, q_low, attn_low, lse, gains, cos2, sin2, block_order,
     )
     e1 = (q_width + k_width) // nf
     e2 = e1 + k_width // nf

time: 487 us -> 479 us (0.984)
  Pallas kernels: 476 us -> 471 us
    pallas_call x1, Pallas kernels: 225 us -> 220 us  [front(): pl.pallas_call(functools.partial(front_kernel, dims), in_specs=[any_] * 5...]
where the time goes in v1:
time: 479 us; the launch traced here: 474 us
  Pallas kernels  471 us (98%)
    pallas_call x1, Pallas kernels, back(): pl.pallas_call(functools.partial(back_kernel, dims), in_specs=[any_] * 16...  237 us
    pallas_call x1, Pallas kernels, front(): pl.pallas_call(functools.partial(front_kernel, dims), in_specs=[any_] * 5...  220 us
    pallas_call x1, Pallas kernels, finish(): pl.pallas_call(functools.partial(finish_kernel, nz, nf, ff, unit, upad, c...  14.3 us

profile of v1, /device:TPU:0, one launch (start us, length us, event | category | flops | bytes accessed | tf_op | source)
XLA Modules:
  0.0 474.1 jit_solution(8687405927630920974)
XLA Ops:
  0.7 0.6 maximum_bitcast_fusion.freq_ref
  1.2 0.8 pad_maximum_fusion
  2.0 0.6 pad.4.sm
  2.6 219.7 %shard_map.177 = (bf16[1536,2048]{1,0:T(8,128)(2,1)}, bf16[1536,1536]{1,0:T(8,128)(2,1)}, bf16[256,1536]{1,0:T(8,128)(2,1)}, bf16[1024,512]{1,0:T(8,128)(2,1)}, ...) custom-call(bf16[192,2048]{1,0:T(8,128)(2,1)} %wq.1, ...), custom_call_target="tpu_custom_call" | custom-call | tf_op jit(solution)/shard_map/pallas_call | solution.py:974
  222.4 237.2 %shard_map.178 = (bf16[256,1536]{1,0:T(8,128)(2,1)}, bf16[256,1536]{1,0:T(8,128)(2,1)}, bf16[1152,1536]{1,0:T(8,128)(2,1)}, bf16[768,2304]{1,0:T(8,128)(2,1)}, b...) custom-call(bf16[1536,4608]{1,0:T(8,128)(2,1)} %get-tuple-element.41.dwgu, ...), custom_call_target="tpu_custom_call" | custom-call | tf_op jit(solution)/shard_map/pallas_call | solution.py:1433
  459.5 14.3 %shard_map.179 = (f32[192,17920]{1,0:T(8,128)}, f32[1120,1536]{1,0:T(8,128)}, f32[192,2048]{1,0:T(8,128)}, f32[192,1536]{1,0:T(8,128)}, bf16[256,1536]{1,0:T(8,1...) custom-call(bf16[768,2304]{1,0:T(8,128)(2,1)} %get-tuple-element.55., ...), custom_call_target="tpu_custom_call" | custom-call | tf_op jit(solution)/shard_map/pallas_call | solution.py:134
  (2 shorter events, 0.0 us)

commit v2 on v1

--- a/solution.py
+++ b/solution.py
@@ -2,6 +2,7 @@
 
 import jax
 import jax.numpy as jnp
+import numpy as np
 from jax import lax
 from jax.experimental import pallas as pl
 from jax.experimental.pallas import tpu as pltpu
@@ -1496,14 +1497,15 @@
     rows = hidden_in.shape[1]
     ff = w_gate_up.shape[1] // 2
     unit = ff // (nf * nz)
-    freqs = THETA ** (-(jnp.arange(HEAD_DIM // 2).astype(F32) * 2.0 / HEAD_DIM))
-    freqs = jnp.concatenate([freqs, freqs])[None]
+    freqs = THETA ** (-(np.arange(HEAD_DIM) % (HEAD_DIM // 2) * 2.0 / HEAD_DIM))
+    freqs = jnp.asarray(freqs[None].astype(np.float32))
     upad = -(-unit // 16) * 16
     wide = nf * upad
     nb, ng = b_qkv.shape[0], gain_attn.shape[0]
     d = hidden_in.shape[2]
     small = jnp.concatenate([b_qkv, gain_attn, gain_mlp])
-    small = jnp.pad(small[None], ((0, 15), (0, -small.shape[0] % 128)))
+    small = jnp.pad(small, (0, -small.shape[0] % 128))
+    small = jnp.broadcast_to(small[None], (16, small.shape[0]))
     grad_low = cotangent[0]
     (whole_qkv, whole_out, q_low, kv_all, attn_low, lse, middle, grad_normed_two, gains, cos2, sin2, gate_up_local, down_part,
      down_own, *_) = front(

time: 479 us -> 479 us (level)
  no operation moved by 1% of the time
where the time goes in v2:
time: 479 us; the launch traced here: 473 us
  Pallas kernels  471 us (98%)
    pallas_call x1, Pallas kernels, back(): pl.pallas_call(functools.partial(back_kernel, dims), in_specs=[any_] * 16...  237 us
    pallas_call x1, Pallas kernels, front(): pl.pallas_call(functools.partial(front_kernel, dims), in_specs=[any_] * 5...  220 us
    pallas_call x1, Pallas kernels, finish(): pl.pallas_call(functools.partial(finish_kernel, nz, nf, ff, unit, upad, c...  14.3 us

profile of v2, /device:TPU:0, one launch (start us, length us, event | category | flops | bytes accessed | tf_op | source)
XLA Modules:
  0.0 473.5 jit_solution(5430578160587151631)
XLA Ops:
  0.6 0.8 pad_maximum_fusion
  1.4 0.6 broadcast_in_dim.12.sm
  2.0 219.7 %shard_map.186 = (bf16[1536,2048]{1,0:T(8,128)(2,1)}, bf16[1536,1536]{1,0:T(8,128)(2,1)}, bf16[256,1536]{1,0:T(8,128)(2,1)}, bf16[1024,512]{1,0:T(8,128)(2,1)}, ...) custom-call(bf16[192,2048]{1,0:T(8,128)(2,1)} %wq.1, ...), custom_call_target="tpu_custom_call" | custom-call | tf_op jit(solution)/shard_map/pallas_call | solution.py:975
  221.8 237.2 %shard_map.187 = (bf16[256,1536]{1,0:T(8,128)(2,1)}, bf16[256,1536]{1,0:T(8,128)(2,1)}, bf16[1152,1536]{1,0:T(8,128)(2,1)}, bf16[768,2304]{1,0:T(8,128)(2,1)}, b...) custom-call(bf16[1536,4608]{1,0:T(8,128)(2,1)} %get-tuple-element.41.dwgu, ...), custom_call_target="tpu_custom_call" | custom-call | tf_op jit(solution)/shard_map/pallas_call | solution.py:1434
  458.9 14.3 %shard_map.188 = (f32[192,17920]{1,0:T(8,128)}, f32[1120,1536]{1,0:T(8,128)}, f32[192,2048]{1,0:T(8,128)}, f32[192,1536]{1,0:T(8,128)}, bf16[256,1536]{1,0:T(8,1...) custom-call(bf16[768,2304]{1,0:T(8,128)(2,1)} %get-tuple-element.55., ...), custom_call_target="tpu_custom_call" | custom-call | tf_op jit(solution)/shard_map/pallas_call | solution.py:135
